TPU v7x, 512 devices: a whole 4x4x16 slice. The times are simulated.
512 devices in a mesh: grp: 64 (over x, y, z_hi), tp: 8 (over z_lo, core).
Axes of the slice: x: 4, y: 4, z: 16 (z_hi: 4, z_lo: 4; z = z_hi * 4 + z_lo), core: 2. Of those that a mesh axis runs over, the one named last changes fastest.
Arguments:
- queries: bfloat16 [8192, 36864], P('grp', 'tp'), may hold values from -64 to 64
- trunk: bfloat16 [512, 576], P('grp'), may hold values from -4 to 4
- own: bfloat16 [8192, 576], P('grp'), may hold values from -6 to 6
- grad_out: bfloat16 [8192, 32768], P('grp', 'tp'), may hold values from -12 to 12
- visible: int32 [8192], P('grp'), may hold values from 2 to 512, as said below
Outputs:
- grad_query: bfloat16 [8192, 36864], P('grp', 'tp')
- grad_trunk: float32 [512, 576], P('grp')
- grad_own: float32 [8192, 576], P('grp')
Inputs may be any that keep to these rules, and one draw needn't show every extreme that they name: `visible`: at least 2, so the first two trunk positions are always seen; the entry of token 0 is 512.
All inputs are finite; a program needn't handle non-finite values.
Results may differ from a plain program's by a relative error of at most 0.0048.
Values may be sent and summed in bfloat16 or wider, within the bound.
A program may use at most 64 MiB of HBM per device.

v0:
```python
import jax
import jax.numpy as jnp
from jax import lax
from jax.sharding import PartitionSpec as P

HL = 512
HR = 64
HK = 576


score_scale = 192.0 ** (-0.5)


def per_device(queries, trunk, own, grad_out, visible):
    rows = queries.shape[0]
    heads = queries.shape[1] // HK
    keys = lax.all_gather(trunk, "grp", axis=0, tiled=True)
    positions = keys.shape[0]
    query3 = queries.reshape(rows, heads, HK)
    grad3 = grad_out.reshape(rows, heads, HL)
    own_f = own.astype(jnp.float32)
    mask = (jnp.arange(positions, dtype=jnp.int32)[None, :] < visible[:, None])[:, None, :]
    scores = (
        jnp.einsum("qhc,kc->qhk", query3, keys, preferred_element_type=jnp.float32) * score_scale
    )
    self_score = (
        jnp.einsum("qhc,qc->qh", query3, own, preferred_element_type=jnp.float32) * score_scale
    )
    scores = jnp.where(mask, scores, jnp.float32(-1e30))
    top = jnp.maximum(jnp.max(scores, axis=-1), self_score)
    expo = jnp.where(mask, jnp.exp(scores - top[..., None]), jnp.float32(0.0))
    self_expo = jnp.exp(self_score - top)
    total = jnp.sum(expo, axis=-1) + self_expo
    prob = expo / total[..., None]
    self_prob = self_expo / total
    dprob = jnp.einsum("qhl,kl->qhk", grad3, keys[:, :HL], preferred_element_type=jnp.float32)
    self_dprob = jnp.einsum("qhl,ql->qh", grad3, own[:, :HL], preferred_element_type=jnp.float32)
    delta = jnp.sum(prob * dprob, axis=-1) + self_prob * self_dprob
    dscore = prob * (dprob - delta[..., None])
    self_dscore = self_prob * (self_dprob - delta)
    prob_b = prob.astype(jnp.bfloat16)
    dscore_b = dscore.astype(jnp.bfloat16)
    grad_q = jnp.einsum("qhk,kc->qhc", dscore_b, keys, preferred_element_type=jnp.float32)
    grad_q = (grad_q + self_dscore[..., None] * own_f[:, None, :]) * score_scale
    grad_query = grad_q.astype(jnp.bfloat16).reshape(rows, heads * HK)
    value_grad = jnp.einsum("qhk,qhl->kl", prob_b, grad3, preferred_element_type=jnp.float32)
    key_grad = (
        jnp.einsum("qhk,qhc->kc", dscore_b, query3, preferred_element_type=jnp.float32)
        * score_scale
    )
    key_grad = key_grad + jnp.pad(value_grad, ((0, 0), (0, HR)))
    own_key = jnp.einsum("qh,qhc->qc", self_dscore, query3.astype(jnp.float32)) * score_scale
    own_value = jnp.einsum("qh,qhl->ql", self_prob, grad3.astype(jnp.float32))
    own_grad = own_key + jnp.pad(own_value, ((0, 0), (0, HR)))
    summed, grad_own = lax.psum((key_grad, own_grad), "tp")
    grad_trunk = lax.psum_scatter(summed, "grp", scatter_dimension=0, tiled=True)
    return (grad_query, grad_trunk, grad_own)


def solution(mesh):
    in_specs = (P("grp", "tp"), P("grp", None), P("grp", None), P("grp", "tp"), P("grp"))
    out_specs = (P("grp", "tp"), P("grp", None), P("grp", None))
    return jax.shard_map(
        per_device, mesh=mesh, in_specs=in_specs, out_specs=out_specs, check_vma=False
    )
```

profile of v0, /device:TPU:1, one launch (start us, length us, event | category | flops | bytes accessed | tf_op | source)
XLA Modules:
  0.0 1171.6 jit_solution(11990737225898741866)
XLA Ops:
  7.2 0.9 convert.1
  8.2 0.9 slice_convert_fusion
  9.1 0.8 iota_compare_fusion
  9.9 1.7 copy.21
  11.6 204.3 %all_gather.3 = bf16[512,576]{1,0:T(8,128)(2,1)S(1)} all-gather(bf16[8,576]{1,0:T(8,128)(2,1)S(1)} %copy-done.8), channel_id=1, replica_groups=mesh['grp'=64,'tp'=8] {'grp'}, dimensions={0}, use_global_device_ids=true | all-gather | bytes 599040 | tf_op jit(solution)/shard_map/all_gather | solution.py:17
  216.1 1.1 fusion
  217.3 0.7 fusion.2
  218.0 1.3 copy-done.2
  219.6 1.7 copy.24
  221.3 4.7 multiply_reduce_fusion.4
  226.0 2.3 convolution_bitcast_fusion.1
  228.8 2.7 multiply_convert_fusion.1
  231.5 1.0 copy-done.4
  232.5 2.1 fusion.4
  234.8 0.7 multiply_reduce_fusion.2
  235.9 0.7 pad_add_fusion
  236.9 0.9 multiply_convert_fusion
  237.8 1.4 copy.26
  239.2 1.3 dynamic-slice
  241.1 807.9 %all-reduce.8.cloned.1.call-done = f32[512,576]{1,0:T(8,128)} async-done(((f32[512,576]{1,0:T(8,128)}), f32[512,576]{1,0:T(8,128)}) %all-reduce.8.cloned.1.call-update) | async-done | bytes 1179664
  1049.0 0.7 constant_dynamic-slice_fusion
  1049.8 62.9 %psum.16 = f32[8,576]{1,0:T(8,128)} all-reduce(f32[8,576]{1,0:T(8,128)S(1)} %constant_dynamic-slice_fusion), channel_id=1, replica_groups=mesh['grp'=64,'tp'=8] {'tp'}, use_global_device_ids=true, to_apply=%region_3.4 | all-reduce | flops 4608 | bytes 36864 | tf_op jit(solution)/shard_map/psum | solution.py:55
  1112.7 50.4 %all-reduce.6.cloned.1.call-done = f32[128,576]{0,1:T(8,128)} async-done(((f32[128,576]{0,1:T(8,128)}), f32[128,576]{0,1:T(8,128)}) %all-reduce.6.cloned.1.call-update) | async-done | bytes 294928 | tf_op jit(solution)/shard_map/psum | solution.py:55
  1163.1 1.7 copy.58
  (34 shorter events, 2.0 us)
Async XLA Ops:
  7.2 4.4 copy-start.8
  7.2 1041.9 %all-reduce.8.cloned.1.call-start = ((), (), s32[]{:S(2)}) async-start(), calls=%async_computation.1 | async-start | bytes 2621440
  215.8 5.5 copy-start.6
  217.2 2.4 copy-start
  217.2 2.0 copy-start.2
  221.3 4.7 copy-start.1
  221.3 4.7 copy-start.3
  228.8 3.7 copy-start.9
  231.5 1.0 copy-start.4
  234.6 928.4 %all-reduce.6.cloned.1.call-start = ((), (), s32[]{:S(2)}) async-start(), calls=%async_computation | async-start | bytes 589824 | tf_op jit(solution)/shard_map/psum | solution.py:55
  234.8 1.9 copy-start.7
  235.6 1.3 copy-start.5
Sparse Core Ops, SparseCore 0:
  234.8 814.2 all-reduce.7
  1052.8 110.2 all-reduce.5
where the time goes:
time: 1170 us
  waiting for transfers between devices  858 us (73%)
  blocking collectives  267 us (23%)
  between operations  14.9 us (1%)
  local copies, waits for them, and re-layouts  11.8 us (1%)
    unnamed x3, waiting for transfers between devices  808 us
    all_gather x1, blocking collectives, per_device(): keys = lax.all_gather(trunk, 'grp', axis=0, tiled=True)  204 us
    psum x1, blocking collectives, per_device(): summed, grad_own = lax.psum((key_grad, own_grad), 'tp')  62.9 us
    psum x1, waiting for transfers between devices, per_device(): summed, grad_own = lax.psum((key_grad, own_grad), 'tp')  50.4 us
  transfers between devices with their start and end apart: 2, of which 2 were waited for; matrix products, arithmetic and copies ran while one was open for 1% of the time, Pallas kernels for 0%

commit v1 on v0

v1 whole, which is shorter than its diff:
```python
import jax
import jax.numpy as jnp
from jax import lax
from jax.experimental import pallas as pl
from jax.experimental.pallas import tpu as pltpu
from jax.sharding import PartitionSpec as P

HL = 512
HR = 64
HK = 576
KP = 640
HEADS = 8
TOK = 128
HALF = 320
MESH = pl.DeviceIdType.MESH
BF = jnp.bfloat16
F32 = jnp.float32

score_scale = 192.0 ** (-0.5)

PLANE = sorted(((dx, dy) for dx in range(4) for dy in range(4) if (dx, dy) != (0, 0)), key=lambda o: (-min(o[0], 4 - o[0]) - min(o[1], 4 - o[1]), o))
FAR_Z = sorted(range(1, 16), key=lambda k: (-min(k, 16 - k), k))


def rows16(start, size):
    return pl.ds(pl.multiple_of(start, 16), size)


def remote(src, dst, send, recv, where):
    return pltpu.make_async_remote_copy(
        src_ref=src, dst_ref=dst, send_sem=send, recv_sem=recv, device_id=where, device_id_type=MESH
    )


def pack(block):
    pad = jnp.zeros((8, 128), F32)
    tail = jnp.concatenate([block[:, 384:640], pad], axis=1)
    return jnp.concatenate([block[:, 0:384], tail], axis=0)


def unpack(block):
    return jnp.concatenate([block[0:8, :], block[8:16, 0:256]], axis=1)


def kernel(
    q_hbm, tr_hbm, own_hbm, g_hbm, vis_hbm,
    gq_hbm, gt_hbm, go_hbm,
    tr_ref, own_ref, vis_ref, gt_ref, got_ref,
    q_s, qo_s, g_s, k_s, bias_s, p_s, d_s, o_s,
    zg_src, zg_buf, kx_src, kx_buf, kacc, xr_src, xr_buf, zr_src, zr_buf, fin_src, fin_buf,
    os_src, oz_buf, ow_buf,
    lq, lo, lg, lw, ls, lf,
    zg_send, zg_recv, xg_send, xg_recv, cg_send, cg_recv, kx_send, kx_recv,
    xr_send, xr_recv, zr_send, zr_recv, fin_send, fin_recv, oz_send, oz_recv, og_send, og_recv, fo_send, fo_recv,
):
    g = lax.axis_index("grp")
    t = lax.axis_index("tp")
    xy, zh = g // 4, g % 4
    zl, core = t // 2, t % 2
    z = zh * 4 + zl
    other = 1 - core
    sib = (g, zl * 2 + other)

    def plane(n, sign):
        dx, dy = PLANE[n]
        return ((xy // 4 + 4 + sign * dx) % 4) * 4 + (xy % 4 + 4 + sign * dy) % 4

    def at_xy(n):
        return (plane(n, 1) * 4 + zh, t)

    def at_z(zz):
        return (xy * 4 + zz // 4, (zz % 4) * 2 + core)

    small = [
        pltpu.make_async_copy(src, dst, ls.at[i])
        for i, (src, dst) in enumerate([(tr_hbm, tr_ref), (own_hbm, own_ref), (vis_hbm, vis_ref)])
    ]
    for copy in small:
        copy.start()

    barrier = pltpu.get_barrier_semaphore()
    for k in FAR_Z:
        pl.semaphore_signal(barrier, inc=1, device_id=at_z((z + k) % 16), device_id_type=MESH)
    for n in range(15):
        pl.semaphore_signal(barrier, inc=1, device_id=at_xy(n), device_id_type=MESH)
    pl.semaphore_signal(barrier, inc=1, device_id=sib, device_id_type=MESH)

    def load_q(hp):
        return pltpu.make_async_copy(
            q_hbm.at[:, pl.ds(hp * 2 * HK, KP)], q_s.at[pl.ds(hp * 256, TOK)], lq.at[hp]
        )

    def load_o(hp):
        return pltpu.make_async_copy(
            q_hbm.at[:, pl.ds(hp * 2 * HK + HL, KP)], qo_s.at[pl.ds(hp * TOK, TOK)], lo.at[hp]
        )

    def load_g(h):
        return pltpu.make_async_copy(
            g_hbm.at[:, pl.ds(h * HL, HL)], g_s.at[pl.ds(h * TOK, TOK)], lg.at[h]
        )

    small[0].wait()
    slab = jnp.concatenate([tr_ref[...].astype(F32), jnp.zeros((8, KP - HK), F32)], axis=1)
    zg_src[...] = pack(slab).astype(BF)
    mine = (zh // 2) == core

    pl.semaphore_wait(barrier, 31)

    def zg(k):
        zz = (zh + k) % 4
        return remote(zg_src, zg_buf.at[zh], zg_send.at[k], zg_recv.at[zh], (xy * 4 + zz, t))

    def zg_from(src):
        return remote(zg_src, zg_buf.at[src], zg_send.at[0], zg_recv.at[src], (g, t))

    @pl.when(mine)
    def _():
        for k in range(1, 4):
            zg(k).start()
        zg_buf[zh] = zg_src[...]

    def zg_sent():
        @pl.when(mine)
        def _():
            for k in range(1, 4):
                zg(k).wait_send()

    drains = [zg_sent]

    for hp in range(HEADS // 2):
        load_q(hp).start()
        load_o(hp).start()
    for h in range(HEADS):
        load_g(h).start()
    small[1].wait()
    owns = own_ref[...].astype(F32).T.astype(BF)
    for cc in range(2):
        k_s[cc * HALF + 256 : (cc + 1) * HALF, :] = jnp.concatenate(
            [owns[cc * 64 : cc * 64 + 64, :], jnp.zeros((64, KP - HK), BF)], axis=1
        )
    small[2].wait()
    seen = vis_ref[...].reshape(1, TOK)
    low = jnp.float32(-1e30)
    for cc in range(2):
        row = lax.broadcasted_iota(jnp.int32, (256, TOK), 0)
        spot = (row // 16) * 32 + cc * 16 + row % 16
        bias_s[cc * HALF : cc * HALF + 256, :] = jnp.where(spot < seen, jnp.float32(0.0), low)
        row = lax.broadcasted_iota(jnp.int32, (64, TOK), 0) + cc * 64
        lane = lax.broadcasted_iota(jnp.int32, (64, TOK), 1)
        bias_s[cc * HALF + 256 : (cc + 1) * HALF, :] = jnp.where(row == lane, jnp.float32(0.0), low)

    for hp in range(HEADS // 2):
        load_q(hp).wait()
        load_o(hp).wait()
        odd = qo_s[hp * TOK : (hp + 1) * TOK, :].astype(F32)
        odd = jnp.concatenate([odd[:, 64:], odd[:, :64]], axis=1)
        q_s[hp * 256 + TOK : hp * 256 + 256, :] = odd.astype(BF)
    for h in range(HEADS):
        load_g(h).wait()

    for i in range(2):
        src = core * 2 + i

        @pl.when(src != zh)
        def _():
            zg_from(src).wait_recv()

    pair = jnp.concatenate([unpack(zg_buf[core * 2 + i].astype(F32)) for i in range(2)], axis=0)
    k_s[rows16(core * HALF + xy * 16, 16), :] = pair.astype(BF)

    def xg(k):
        block = k_s.at[rows16(core * HALF + xy * 16, 16)]
        return remote(block, block, xg_send.at[k], xg_recv.at[k], at_xy(k))

    def cg(n):
        spot = xy if n == 15 else plane(n, -1)
        block = k_s.at[rows16(core * HALF + spot * 16, 16)]
        return remote(block, block, cg_send.at[n], cg_recv.at[n], sib)

    def xg_got(n):
        block = k_s.at[rows16(core * HALF + plane(n, -1) * 16, 16)]
        return remote(block, block, xg_send.at[n], xg_recv.at[n], at_xy(n))

    def cg_got(n):
        spot = xy if n == 15 else plane(n, -1)
        block = k_s.at[rows16(other * HALF + spot * 16, 16)]
        return remote(block, block, cg_send.at[n], cg_recv.at[n], sib)

    for n in range(15):
        xg(n).start()
    cg(15).start()
    for n in reversed(range(15)):
        xg_got(n).wait_recv()
        cg(n).start()
    for n in reversed(range(16)):
        cg_got(n).wait_recv()

    def keys_sent():
        cg(15).wait_send()
        for n in range(15):
            xg(n).wait_send()
            cg(n).wait_send()

    drains.append(keys_sent)


    for hp in range(HEADS // 2):
        at = slice(hp * 256, hp * 256 + 256)
        nt = (((1,), (1,)), ((), ()))
        s = lax.dot_general(k_s[...], q_s[at, :], nt, preferred_element_type=F32)
        dp = lax.dot_general(k_s[:, 0:HL], g_s[at, :], nt, preferred_element_type=F32)
        bias = jnp.concatenate([bias_s[...], bias_s[...]], axis=1)
        s = s * score_scale + bias
        top = jnp.max(s, axis=0, keepdims=True)
        e = jnp.exp(s - top)
        inv = 1.0 / jnp.sum(e, axis=0, keepdims=True)
        p = e * inv
        delta = jnp.sum(p * dp, axis=0, keepdims=True)
        p_s[:, at] = p.astype(BF)
        d_s[:, at] = (p * (dp - delta)).astype(BF)

    def key_grad(half):
        at = rows16(half * HALF, HALF)
        a = jnp.dot(d_s[at, :], q_s[...], preferred_element_type=F32) * score_scale
        b = jnp.dot(p_s[at, :], g_s[...], preferred_element_type=F32)
        return jnp.concatenate([a[:, 0:HL] + b, a[:, HL:]], axis=1)

    kx_src[...] = key_grad(other).astype(BF)
    kx = remote(kx_src, kx_buf, kx_send, kx_recv, sib)
    kx.start()
    drains.append(kx.wait_send)
    kacc[...] = key_grad(core)
    kx.wait_recv()
    total = kacc[...] + kx_buf[...].astype(F32)
    kacc[...] = total
    xr_src[...] = total[0:256, :].astype(BF)
    os_src[...] = total[256:HALF, :].astype(BF)

    def xr(n):
        block = xr_src.at[rows16(plane(n, 1) * 16, 16)]
        return remote(block, xr_buf.at[n], xr_send.at[n], xr_recv.at[n], at_xy(n))

    for n in range(15):
        xr(n).start()

    def oz(k):
        to = (zl + k) % 4
        return remote(os_src.at[rows16(to * 16, 16)], oz_buf.at[zl], oz_send.at[k], oz_recv.at[zl], (g, to * 2 + core))

    def oz_from(k):
        src = (zl + k) % 4
        return remote(os_src.at[0:16], oz_buf.at[src], oz_send.at[k], oz_recv.at[src], (g, src * 2 + core))

    def og(k):
        block = ow_buf.at[rows16(core * 64 + zl * 16, 16)]
        return remote(block, block, og_send.at[k], og_recv.at[zl], (g, ((zl + k) % 4) * 2 + core))

    def og_from(k):
        src = (zl + k) % 4
        block = ow_buf.at[rows16(core * 64 + src * 16, 16)]
        return remote(block, block, og_send.at[k], og_recv.at[src], (g, src * 2 + core))

    for k in range(1, 4):
        oz(k).start()
    oz_buf[zl] = os_src[rows16(zl * 16, 16), :]

    def sums_sent():
        for n in range(15):
            xr(n).wait_send()
        for k in range(1, 4):
            oz(k).wait_send()

    drains.append(sums_sent)

    def store_q(hp):
        return pltpu.make_async_copy(
            o_s.at[:, pl.ds(pl.multiple_of(hp * 2 * HK, 128), 2 * HK)],
            gq_hbm.at[:, pl.ds(pl.multiple_of(hp * 2 * HK, 128), 2 * HK)],
            lw.at[hp],
        )

    @pl.loop(0, HEADS // 2)
    def _(hp):
        at = pl.ds(pl.multiple_of(hp * 256, 256), 256)
        tn = (((0,), (0,)), ((), ()))
        gq = lax.dot_general(d_s[:, at], k_s[...], tn, preferred_element_type=F32) * score_scale
        even, odd = gq[0:TOK, :], gq[TOK:, :]
        odd = jnp.concatenate([odd[:, HK:], odd[:, :HK]], axis=1)
        joint = jnp.concatenate([even[:, 0:HL], even[:, HL:] + odd[:, 0:128], odd[:, 128:]], axis=1)
        o_s[:, pl.ds(pl.multiple_of(hp * 2 * HK, 128), 2 * HK)] = joint.astype(BF)
        store_q(hp).start()

    drains.append(lambda: [store_q(hp).wait() for hp in range(HEADS // 2)])
    for k in range(1, 4):
        oz_from(k).wait_recv()
    own_sum = oz_buf[0].astype(F32)
    for a in range(1, 4):
        own_sum = own_sum + oz_buf[a].astype(F32)
    ow_buf[rows16(core * 64 + zl * 16, 16), :] = own_sum.astype(BF)
    for k in range(1, 4):
        og(k).start()
    drains.append(lambda: [og(k).wait_send() for k in range(1, 4)])

    total = kacc[rows16(xy * 16, 16), :]
    for n in reversed(range(15)):
        xr(n).wait_recv()
        total = total + xr_buf[n].astype(F32)
    zr_src[0] = pack(total[0:8, :]).astype(BF)
    zr_src[1] = pack(total[8:16, :]).astype(BF)

    def zr(i, a):
        to = (core * 2 + i) * 4 + a
        return remote(zr_src.at[i], zr_buf.at[z], zr_send.at[i * 4 + a], zr_recv.at[z], at_z(to))

    def zr_from(src):
        return remote(zr_src.at[0], zr_buf.at[src], zr_send.at[0], zr_recv.at[src], at_z(src))

    for i in range(2):
        for a in range(4):

            @pl.when((core * 2 + i) * 4 + a != z)
            def _():
                zr(i, a).start()

    def slabs_sent():
        for i in range(2):
            for a in range(4):

                @pl.when((core * 2 + i) * 4 + a != z)
                def _():
                    zr(i, a).wait_send()

    drains.append(slabs_sent)

    for k in range(1, 4):
        og_from(k).wait_recv()
    own_half = ow_buf.at[rows16(core * 64, 64)]
    fo = remote(own_half, own_half, fo_send, fo_recv, sib)
    fo.start()
    drains.append(fo.wait_send)
    own_half = ow_buf.at[rows16(other * 64, 64)]
    remote(own_half, own_half, fo_send, fo_recv, sib).wait_recv()
    got_ref[...] = ow_buf[...].astype(F32).T[0:HK, :]
    store_go = pltpu.make_async_copy(got_ref, go_hbm, lf.at[0])
    store_go.start()
    drains.append(store_go.wait)

    fin = remote(fin_src, fin_buf, fin_send, fin_recv, sib)

    @pl.when(mine)
    def _():
        zr_buf[z] = zr_src[zh % 2]
        total = jnp.zeros((16, 384), F32)
        for src in range(16):

            @pl.when(z != src)
            def _():
                zr_from(src).wait_recv()

            total = total + zr_buf[src].astype(F32)
        whole = unpack(total)
        fin_src[...] = whole
        fin.start()
        gt_ref[...] = whole[:, 0:HK]
        fin.wait_send()

    @pl.when(jnp.logical_not(mine))
    def _():
        fin.wait_recv()
        gt_ref[...] = fin_buf[:, 0:HK]

    store_gt = pltpu.make_async_copy(gt_ref, gt_hbm, lf.at[1])
    store_gt.start()
    drains.append(store_gt.wait)

    for drain in drains:
        drain()


def finish(q_in, t_in, o_in, q_out, t_out, o_out, q_s, t_s, o_s, sem, sem_out):
    pieces = [(q_in.at[pl.ds(i * 32, 32)], q_s.at[pl.ds(i * 32, 32)], q_out.at[pl.ds(i * 32, 32)]) for i in range(4)]
    pieces += [(o_in, o_s, o_out), (t_in, t_s, t_out)]
    loads = [pltpu.make_async_copy(p[0], p[1], sem.at[i]) for i, p in enumerate(pieces)]
    stores = [pltpu.make_async_copy(p[1], p[2], sem_out.at[i]) for i, p in enumerate(pieces)]
    for c in loads:
        c.start()
    for load, store in zip(loads, stores):
        load.wait()
        store.start()
    for c in stores:
        c.wait()


def per_device(queries, trunk, own, grad_out, visible):
    hbm = pl.BlockSpec(memory_space=pl.ANY)
    dma = pltpu.SemaphoreType.DMA
    grad_query, grad_trunk, grad_own = pl.pallas_call(
        kernel,
        out_shape=(
            jax.ShapeDtypeStruct((TOK, HEADS * HK), BF),
            jax.ShapeDtypeStruct((8, HK), F32),
            jax.ShapeDtypeStruct((HK, TOK), F32),
        ),
        in_specs=[hbm] * 5,
        out_specs=(hbm,) * 3,
        scratch_shapes=[
            pltpu.VMEM((8, HK), BF),
            pltpu.VMEM((HK, TOK), BF),
            pltpu.VMEM((TOK,), jnp.int32),
            pltpu.VMEM((8, HK), F32),
            pltpu.VMEM((HK, TOK), F32),
            pltpu.VMEM((HEADS * TOK, KP), BF),
            pltpu.VMEM((HEADS // 2 * TOK, KP), BF),
            pltpu.VMEM((HEADS * TOK, HL), BF),
            pltpu.VMEM((2 * HALF, KP), BF),
            pltpu.VMEM((2 * HALF, TOK), F32),
            pltpu.VMEM((2 * HALF, HEADS * TOK), BF),
            pltpu.VMEM((2 * HALF, HEADS * TOK), BF),
            pltpu.VMEM((TOK, HEADS * HK), BF),
            pltpu.VMEM((16, 384), BF),
            pltpu.VMEM((4, 16, 384), BF),
            pltpu.VMEM((HALF, KP), BF),
            pltpu.VMEM((HALF, KP), BF),
            pltpu.VMEM((HALF, KP), F32),
            pltpu.VMEM((256, KP), BF),
            pltpu.VMEM((16, 16, KP), BF),
            pltpu.VMEM((2, 16, 384), BF),
            pltpu.VMEM((16, 16, 384), BF),
            pltpu.VMEM((8, KP), F32),
            pltpu.VMEM((8, KP), F32),
            pltpu.VMEM((64, KP), BF),
            pltpu.VMEM((4, 16, KP), BF),
            pltpu.VMEM((TOK, KP), BF),
            dma((4,)), dma((4,)), dma((8,)), dma((4,)), dma((3,)), dma((2,)),
            dma((4,)), dma((4,)),
            dma((16,)), dma((16,)),
            dma((16,)), dma((16,)),
            dma, dma,
            dma((16,)), dma((16,)),
            dma((8,)), dma((16,)),
            dma, dma,
            dma((4,)), dma((4,)), dma((4,)), dma((4,)),
            dma, dma,
        ],
        compiler_params=pltpu.CompilerParams(
            collective_id=0, has_side_effects=True, vmem_limit_bytes=60 * 1024 * 1024
        ),
        cost_estimate=pl.CostEstimate(flops=3860000000, bytes_accessed=4500000, transcendentals=655360),
    )(queries, trunk, own.T, grad_out, visible)
    outs = [jax.ShapeDtypeStruct(a.shape, a.dtype) for a in (grad_query, grad_trunk, grad_own)]
    grad_query, grad_trunk, grad_own = pl.pallas_call(
        finish,
        out_shape=outs,
        in_specs=[hbm] * 3,
        out_specs=[hbm] * 3,
        scratch_shapes=[pltpu.VMEM(a.shape, a.dtype) for a in outs] + [dma((6,)), dma((6,))],
        compiler_params=pltpu.CompilerParams(vmem_limit_bytes=60 * 1024 * 1024),
    )(grad_query, grad_trunk, grad_own)
    return grad_query, grad_trunk, grad_own.T


def solution(mesh):
    in_specs = (P("grp", "tp"), P("grp", None), P("grp", None), P("grp", "tp"), P("grp"))
    out_specs = (P("grp", "tp"), P("grp", None), P("grp", None))
    return jax.shard_map(
        per_device, mesh=mesh, in_specs=in_specs, out_specs=out_specs, check_vma=False
    )
```

time: 1170 us -> 57.7 us (0.05)
  waiting for transfers between devices: 858 us -> 0 us
  blocking collectives: 267 us -> 0 us
  Pallas kernels: 0 us -> 56.9 us
  between operations: 14.9 us -> 0.64 us
  local copies, waits for them, and re-layouts: 11.8 us -> 0 us
    unnamed x3 -> x0, waiting for transfers between devices: 808 us -> none
    all_gather x1 -> x0, blocking collectives: 204 us -> none  [per_device(): keys = lax.all_gather(trunk, 'grp', axis=0, tiled=True)]
    psum x1 -> x0, blocking collectives: 62.9 us -> none  [per_device(): summed, grad_own = lax.psum((key_grad, own_grad), 'tp')]
    pallas_call x0 -> x2, Pallas kernels: none -> 56.9 us  [the longest x1 54.7 us: per_device(): pl.pallas_call(kernel, out_shape=(jax.ShapeDtypeStruct((TOK, HEADS * HK),...]
    psum x1 -> x0, waiting for transfers between devices: 50.4 us -> none  [per_device(): summed, grad_own = lax.psum((key_grad, own_grad), 'tp')]
  transfers between devices with their start and end apart: 2 -> 0, of which waited for: 2 -> 0; matrix products, arithmetic and copies ran while one was open for 1% -> 0% of each run, Pallas kernels for 0% -> 0%
where the time goes in v1:
time: 57.7 us; the launch traced here: 57.5 us
  Pallas kernels  56.9 us (99%)
  between operations  0.64 us (1%)
    pallas_call x1, Pallas kernels, per_device(): pl.pallas_call(kernel, out_shape=(jax.ShapeDtypeStruct((TOK, HEADS * HK),...  54.7 us
    pallas_call x1, Pallas kernels, per_device(): pl.pallas_call(finish, out_shape=outs, in_specs=[hbm] * 3, out_specs=[hbm...  2.17 us

profile of v1, /device:TPU:1, one launch (start us, length us, event | category | flops | bytes accessed | tf_op | source)
XLA Modules:
  0.0 57.5 jit_solution(154138660430486244)
XLA Ops:
  0.6 54.7 %shard_map.76 = (bf16[128,4608]{1,0:T(8,128)(2,1)}, f32[8,576]{1,0:T(8,128)}, f32[576,128]{1,0:T(8,128)}) custom-call(bf16[128,4608]{1,0:T(8,128)(2,1)} %q_hbm.1, bf16[8,576]{1,0:T(8,128)(2,1)} %tr_hbm.1, bf16[576,128]{1,0:T(8,128)(2,1)} %bitcast.3, bf16[128,4096]{1,0:T(8,128)(2,1)} %g_hbm.1, s32[128]{0:T(128)} %vis_hbm.1), custom_call_target="tpu_custom_call" | custom-call | flops 3860000000 | bytes 4500000 | tf_op jit(solution)/shard_map/pallas_call | solution.py:398
  55.3 2.2 %shard_map.77 = (bf16[128,4608]{1,0:T(8,128)(2,1)}, f32[8,576]{1,0:T(8,128)}, f32[576,128]{1,0:T(8,128)}) custom-call(bf16[128,4608]{1,0:T(8,128)(2,1)} %get-tuple-element.9.q_in, f32[8,576]{1,0:T(8,128)} %get-tuple-element.10.t_in, f32[576,128]{1,0:T(8,128)} %get-tuple-element.11.o_in), custom_call_target="tpu_custom_call" | custom-call | tf_op jit(solution)/shard_map/pallas_call | solution.py:452

commit v2 on v1

--- a/solution.py
+++ b/solution.py
@@ -19,7 +19,7 @@
 score_scale = 192.0 ** (-0.5)
 
 PLANE = sorted(((dx, dy) for dx in range(4) for dy in range(4) if (dx, dy) != (0, 0)), key=lambda o: (-min(o[0], 4 - o[0]) - min(o[1], 4 - o[1]), o))
-FAR_Z = sorted(range(1, 16), key=lambda k: (-min(k, 16 - k), k))
+NEAR_Z = sorted((d for d in range(1, 16) if d < 7 or d > 9), key=lambda k: (-min(k, 16 - k), k))
 
 
 def rows16(start, size):
@@ -46,12 +46,12 @@
     q_hbm, tr_hbm, own_hbm, g_hbm, vis_hbm,
     gq_hbm, gt_hbm, go_hbm,
     tr_ref, own_ref, vis_ref, gt_ref, got_ref,
-    q_s, qo_s, g_s, k_s, bias_s, p_s, d_s, o_s,
+    q_s, qo_s, g_s, k_s, bias_s, s_s, dp_s, p_s, d_s, o_s,
     zg_src, zg_buf, kx_src, kx_buf, kacc, xr_src, xr_buf, zr_src, zr_buf, fin_src, fin_buf,
     os_src, oz_buf, ow_buf,
     lq, lo, lg, lw, ls, lf,
     zg_send, zg_recv, xg_send, xg_recv, cg_send, cg_recv, kx_send, kx_recv,
-    xr_send, xr_recv, zr_send, zr_recv, fin_send, fin_recv, oz_send, oz_recv, og_send, og_recv, fo_send, fo_recv,
+    xr_send, xr_recv, zr_send, zr_recv, fin_send, fin_recv, oz_send, oz_recv, og_send, og_recv, fo_send, fo_recv, relay,
 ):
     g = lax.axis_index("grp")
     t = lax.axis_index("tp")
@@ -79,7 +79,7 @@
         copy.start()
 
     barrier = pltpu.get_barrier_semaphore()
-    for k in FAR_Z:
+    for k in NEAR_Z:
         pl.semaphore_signal(barrier, inc=1, device_id=at_z((z + k) % 16), device_id_type=MESH)
     for n in range(15):
         pl.semaphore_signal(barrier, inc=1, device_id=at_xy(n), device_id_type=MESH)
@@ -105,28 +105,37 @@
     zg_src[...] = pack(slab).astype(BF)
     mine = (zh // 2) == core
 
-    pl.semaphore_wait(barrier, 31)
-
-    def zg(k):
-        zz = (zh + k) % 4
-        return remote(zg_src, zg_buf.at[zh], zg_send.at[k], zg_recv.at[zh], (xy * 4 + zz, t))
+    pl.semaphore_wait(barrier, 28)
+
+    def zg(d, up):
+        zz = (z + d) % 16 if up else (z + 16 - d) % 16
+        return remote(zg_src, zg_buf.at[zh], zg_send.at[d], zg_recv.at[zh], at_z(zz))
 
     def zg_from(src):
         return remote(zg_src, zg_buf.at[src], zg_send.at[0], zg_recv.at[src], (g, t))
 
+    for chip, up in ((3, True), (0, False)):
+
+        @pl.when(jnp.logical_and(mine, zl == chip))
+        def _():
+            for d in reversed(range(1, 7)):
+                zg(d, up).start()
+
     @pl.when(mine)
     def _():
-        for k in range(1, 4):
-            zg(k).start()
         zg_buf[zh] = zg_src[...]
 
     def zg_sent():
-        @pl.when(mine)
-        def _():
-            for k in range(1, 4):
-                zg(k).wait_send()
+        for chip, up in ((3, True), (0, False)):
+
+            @pl.when(jnp.logical_and(mine, zl == chip))
+            def _():
+                for d in range(1, 7):
+                    zg(d, up).wait_send()
 
     drains = [zg_sent]
+
+    pl.semaphore_signal(relay, inc=1, device_id=at_z((z + 10) % 16), device_id_type=MESH)
 
     for hp in range(HEADS // 2):
         load_q(hp).start()
@@ -193,9 +202,6 @@
     for n in reversed(range(15)):
         xg_got(n).wait_recv()
         cg(n).start()
-    for n in reversed(range(16)):
-        cg_got(n).wait_recv()
-
     def keys_sent():
         cg(15).wait_send()
         for n in range(15):
@@ -204,21 +210,35 @@
 
     drains.append(keys_sent)
 
+    nt = (((1,), (1,)), ((), ()))
+    own_rows, other_rows = rows16(core * HALF, HALF), rows16(other * HALF, HALF)
+
+    def scores(rows, at):
+        s = lax.dot_general(k_s[rows, :], q_s[at, :], nt, preferred_element_type=F32)
+        dp = lax.dot_general(k_s[rows, 0:HL], g_s[at, :], nt, preferred_element_type=F32)
+        bias = jnp.concatenate([bias_s[rows, :], bias_s[rows, :]], axis=1)
+        return s * score_scale + bias, dp
 
     for hp in range(HEADS // 2):
         at = slice(hp * 256, hp * 256 + 256)
-        nt = (((1,), (1,)), ((), ()))
-        s = lax.dot_general(k_s[...], q_s[at, :], nt, preferred_element_type=F32)
-        dp = lax.dot_general(k_s[:, 0:HL], g_s[at, :], nt, preferred_element_type=F32)
-        bias = jnp.concatenate([bias_s[...], bias_s[...]], axis=1)
-        s = s * score_scale + bias
-        top = jnp.max(s, axis=0, keepdims=True)
-        e = jnp.exp(s - top)
-        inv = 1.0 / jnp.sum(e, axis=0, keepdims=True)
-        p = e * inv
-        delta = jnp.sum(p * dp, axis=0, keepdims=True)
-        p_s[:, at] = p.astype(BF)
-        d_s[:, at] = (p * (dp - delta)).astype(BF)
+        s_s[:, at], dp_s[:, at] = scores(own_rows, at)
+
+    for n in reversed(range(16)):
+        cg_got(n).wait_recv()
+
+    for hp in range(HEADS // 2):
+        at = slice(hp * 256, hp * 256 + 256)
+        s1, dp1 = scores(other_rows, at)
+        s0, dp0 = s_s[:, at], dp_s[:, at]
+        top = jnp.maximum(jnp.max(s0, axis=0, keepdims=True), jnp.max(s1, axis=0, keepdims=True))
+        e0, e1 = jnp.exp(s0 - top), jnp.exp(s1 - top)
+        inv = 1.0 / (jnp.sum(e0, axis=0, keepdims=True) + jnp.sum(e1, axis=0, keepdims=True))
+        p0, p1 = e0 * inv, e1 * inv
+        delta = jnp.sum(p0 * dp0, axis=0, keepdims=True) + jnp.sum(p1 * dp1, axis=0, keepdims=True)
+        p_s[own_rows, at] = p0.astype(BF)
+        p_s[other_rows, at] = p1.astype(BF)
+        d_s[own_rows, at] = (p0 * (dp0 - delta)).astype(BF)
+        d_s[other_rows, at] = (p1 * (dp1 - delta)).astype(BF)
 
     def key_grad(half):
         at = rows16(half * HALF, HALF)
@@ -308,6 +328,8 @@
         total = total + xr_buf[n].astype(F32)
     zr_src[0] = pack(total[0:8, :]).astype(BF)
     zr_src[1] = pack(total[8:16, :]).astype(BF)
+
+    pl.semaphore_wait(relay, 1)
 
     def zr(i, a):
         to = (core * 2 + i) * 4 + a
@@ -415,6 +437,8 @@
             pltpu.VMEM((HEADS * TOK, HL), BF),
             pltpu.VMEM((2 * HALF, KP), BF),
             pltpu.VMEM((2 * HALF, TOK), F32),
+            pltpu.VMEM((HALF, HEADS * TOK), F32),
+            pltpu.VMEM((HALF, HEADS * TOK), F32),
             pltpu.VMEM((2 * HALF, HEADS * TOK), BF),
             pltpu.VMEM((2 * HALF, HEADS * TOK), BF),
             pltpu.VMEM((TOK, HEADS * HK), BF),
@@ -433,7 +457,7 @@
             pltpu.VMEM((4, 16, KP), BF),
             pltpu.VMEM((TOK, KP), BF),
             dma((4,)), dma((4,)), dma((8,)), dma((4,)), dma((3,)), dma((2,)),
-            dma((4,)), dma((4,)),
+            dma((8,)), dma((4,)),
             dma((16,)), dma((16,)),
             dma((16,)), dma((16,)),
             dma, dma,
@@ -442,6 +466,7 @@
             dma, dma,
             dma((4,)), dma((4,)), dma((4,)), dma((4,)),
             dma, dma,
+            pltpu.SemaphoreType.REGULAR,
         ],
         compiler_params=pltpu.CompilerParams(
             collective_id=0, has_side_effects=True, vmem_limit_bytes=60 * 1024 * 1024

time: 57.7 us -> 55.5 us (0.962)
  Pallas kernels: 56.9 us -> 54.7 us
    pallas_call x1, Pallas kernels: 54.7 us -> 52.5 us  [per_device(): pl.pallas_call(kernel, out_shape=(jax.ShapeDtypeStruct((TOK, HEADS * HK),...]
where the time goes in v2:
time: 55.5 us; the launch traced here: 55.4 us
  Pallas kernels  54.7 us (99%)
  between operations  0.64 us (1%)
    pallas_call x1, Pallas kernels, per_device(): pl.pallas_call(kernel, out_shape=(jax.ShapeDtypeStruct((TOK, HEADS * HK),...  52.5 us
    pallas_call x1, Pallas kernels, per_device(): pl.pallas_call(finish, out_shape=outs, in_specs=[hbm] * 3, out_specs=[hbm...  2.17 us

profile of v2, /device:TPU:1, one launch (start us, length us, event | category | flops | bytes accessed | tf_op | source)
XLA Modules:
  0.0 55.4 jit_solution(9785361315699418491)
XLA Ops:
  0.6 52.5 %shard_map.76 = (bf16[128,4608]{1,0:T(8,128)(2,1)}, f32[8,576]{1,0:T(8,128)}, f32[576,128]{1,0:T(8,128)}) custom-call(bf16[128,4608]{1,0:T(8,128)(2,1)} %q_hbm.1, bf16[8,576]{1,0:T(8,128)(2,1)} %tr_hbm.1, bf16[576,128]{1,0:T(8,128)(2,1)} %bitcast.3, bf16[128,4096]{1,0:T(8,128)(2,1)} %g_hbm.1, s32[128]{0:T(128)} %vis_hbm.1), custom_call_target="tpu_custom_call" | custom-call | flops 3860000000 | bytes 4500000 | tf_op jit(solution)/shard_map/pallas_call | solution.py:420
  53.2 2.2 %shard_map.77 = (bf16[128,4608]{1,0:T(8,128)(2,1)}, f32[8,576]{1,0:T(8,128)}, f32[576,128]{1,0:T(8,128)}) custom-call(bf16[128,4608]{1,0:T(8,128)(2,1)} %get-tuple-element.9.q_in, f32[8,576]{1,0:T(8,128)} %get-tuple-element.10.t_in, f32[576,128]{1,0:T(8,128)} %get-tuple-element.11.o_in), custom_call_target="tpu_custom_call" | custom-call | tf_op jit(solution)/shard_map/pallas_call | solution.py:477

commit v3 on v2

--- a/solution.py
+++ b/solution.py
@@ -11,12 +11,14 @@
 KP = 640
 HEADS = 8
 TOK = 128
-HALF = 320
+HALF = 256
+ROWS = 640
 MESH = pl.DeviceIdType.MESH
 BF = jnp.bfloat16
 F32 = jnp.float32
 
 score_scale = 192.0 ** (-0.5)
+log2e = 1.4426950408889634
 
 PLANE = sorted(((dx, dy) for dx in range(4) for dy in range(4) if (dx, dy) != (0, 0)), key=lambda o: (-min(o[0], 4 - o[0]) - min(o[1], 4 - o[1]), o))
 NEAR_Z = sorted((d for d in range(1, 16) if d < 7 or d > 9), key=lambda k: (-min(k, 16 - k), k))
@@ -47,10 +49,10 @@
     gq_hbm, gt_hbm, go_hbm,
     tr_ref, own_ref, vis_ref, gt_ref, got_ref,
     q_s, qo_s, g_s, k_s, bias_s, s_s, dp_s, p_s, d_s, o_s,
-    zg_src, zg_buf, kx_src, kx_buf, kacc, xr_src, xr_buf, zr_src, zr_buf, fin_src, fin_buf,
+    zg_src, zg_buf, kx_src, kx_buf, kacc, ko_src, ko_buf, ko_acc, xr_src, xr_buf, zr_src, zr_buf, fin_src, fin_buf,
     os_src, oz_buf, ow_buf,
     lq, lo, lg, lw, ls, lf,
-    zg_send, zg_recv, xg_send, xg_recv, cg_send, cg_recv, kx_send, kx_recv,
+    zg_send, zg_recv, xg_send, xg_recv, cg_send, cg_recv, kx_send, kx_recv, ko_send, ko_recv,
     xr_send, xr_recv, zr_send, zr_recv, fin_send, fin_recv, oz_send, oz_recv, og_send, og_recv, fo_send, fo_recv, relay,
 ):
     g = lax.axis_index("grp")
@@ -144,20 +146,17 @@
         load_g(h).start()
     small[1].wait()
     owns = own_ref[...].astype(F32).T.astype(BF)
-    for cc in range(2):
-        k_s[cc * HALF + 256 : (cc + 1) * HALF, :] = jnp.concatenate(
-            [owns[cc * 64 : cc * 64 + 64, :], jnp.zeros((64, KP - HK), BF)], axis=1
-        )
+    k_s[2 * HALF : ROWS, :] = jnp.concatenate([owns, jnp.zeros((TOK, KP - HK), BF)], axis=1)
     small[2].wait()
     seen = vis_ref[...].reshape(1, TOK)
     low = jnp.float32(-1e30)
     for cc in range(2):
-        row = lax.broadcasted_iota(jnp.int32, (256, TOK), 0)
+        row = lax.broadcasted_iota(jnp.int32, (HALF, TOK), 0)
         spot = (row // 16) * 32 + cc * 16 + row % 16
-        bias_s[cc * HALF : cc * HALF + 256, :] = jnp.where(spot < seen, jnp.float32(0.0), low)
-        row = lax.broadcasted_iota(jnp.int32, (64, TOK), 0) + cc * 64
-        lane = lax.broadcasted_iota(jnp.int32, (64, TOK), 1)
-        bias_s[cc * HALF + 256 : (cc + 1) * HALF, :] = jnp.where(row == lane, jnp.float32(0.0), low)
+        bias_s[cc * HALF : (cc + 1) * HALF, :] = jnp.where(spot < seen, jnp.float32(0.0), low)
+    row = lax.broadcasted_iota(jnp.int32, (TOK, TOK), 0)
+    lane = lax.broadcasted_iota(jnp.int32, (TOK, TOK), 1)
+    bias_s[2 * HALF : ROWS, :] = jnp.where(row == lane, jnp.float32(0.0), low)
 
     for hp in range(HEADS // 2):
         load_q(hp).wait()
@@ -168,6 +167,18 @@
     for h in range(HEADS):
         load_g(h).wait()
 
+    nt = (((1,), (1,)), ((), ()))
+
+    def scores(rows):
+        for hp in range(HEADS // 2):
+            at = slice(hp * 256, hp * 256 + 256)
+            s = lax.dot_general(k_s[rows, :], q_s[at, :], nt, preferred_element_type=F32)
+            bias = jnp.concatenate([bias_s[rows, :], bias_s[rows, :]], axis=1)
+            s_s[rows, at] = s * (score_scale * log2e) + bias
+            dp_s[rows, at] = lax.dot_general(k_s[rows, 0:HL], g_s[at, :], nt, preferred_element_type=F32)
+
+    scores(slice(2 * HALF, ROWS))
+
     for i in range(2):
         src = core * 2 + i
 
@@ -180,21 +191,16 @@
 
     def xg(k):
         block = k_s.at[rows16(core * HALF + xy * 16, 16)]
-        return remote(block, block, xg_send.at[k], xg_recv.at[k], at_xy(k))
+        return remote(block, block, xg_send, xg_recv.at[k], at_xy(k))
 
     def cg(n):
         spot = xy if n == 15 else plane(n, -1)
         block = k_s.at[rows16(core * HALF + spot * 16, 16)]
-        return remote(block, block, cg_send.at[n], cg_recv.at[n], sib)
+        return remote(block, block, cg_send, cg_recv, sib)
 
     def xg_got(n):
         block = k_s.at[rows16(core * HALF + plane(n, -1) * 16, 16)]
-        return remote(block, block, xg_send.at[n], xg_recv.at[n], at_xy(n))
-
-    def cg_got(n):
-        spot = xy if n == 15 else plane(n, -1)
-        block = k_s.at[rows16(other * HALF + spot * 16, 16)]
-        return remote(block, block, cg_send.at[n], cg_recv.at[n], sib)
+        return remote(block, block, xg_send, xg_recv.at[n], at_xy(n))
 
     for n in range(15):
         xg(n).start()
@@ -202,64 +208,53 @@
     for n in reversed(range(15)):
         xg_got(n).wait_recv()
         cg(n).start()
+    own_rows, other_rows = rows16(core * HALF, HALF), rows16(other * HALF, HALF)
+
     def keys_sent():
-        cg(15).wait_send()
-        for n in range(15):
-            xg(n).wait_send()
-            cg(n).wait_send()
+        most = k_s.at[0:240]
+        remote(most, most, xg_send, xg_recv.at[0], sib).wait_send()
+        half = k_s.at[own_rows]
+        remote(half, half, cg_send, cg_recv, sib).wait_send()
 
     drains.append(keys_sent)
 
-    nt = (((1,), (1,)), ((), ()))
-    own_rows, other_rows = rows16(core * HALF, HALF), rows16(other * HALF, HALF)
-
-    def scores(rows, at):
-        s = lax.dot_general(k_s[rows, :], q_s[at, :], nt, preferred_element_type=F32)
-        dp = lax.dot_general(k_s[rows, 0:HL], g_s[at, :], nt, preferred_element_type=F32)
-        bias = jnp.concatenate([bias_s[rows, :], bias_s[rows, :]], axis=1)
-        return s * score_scale + bias, dp
+    scores(own_rows)
+    half = k_s.at[other_rows]
+    remote(half, half, cg_send, cg_recv, sib).wait_recv()
+    scores(other_rows)
 
     for hp in range(HEADS // 2):
         at = slice(hp * 256, hp * 256 + 256)
-        s_s[:, at], dp_s[:, at] = scores(own_rows, at)
-
-    for n in reversed(range(16)):
-        cg_got(n).wait_recv()
-
-    for hp in range(HEADS // 2):
-        at = slice(hp * 256, hp * 256 + 256)
-        s1, dp1 = scores(other_rows, at)
-        s0, dp0 = s_s[:, at], dp_s[:, at]
-        top = jnp.maximum(jnp.max(s0, axis=0, keepdims=True), jnp.max(s1, axis=0, keepdims=True))
-        e0, e1 = jnp.exp(s0 - top), jnp.exp(s1 - top)
-        inv = 1.0 / (jnp.sum(e0, axis=0, keepdims=True) + jnp.sum(e1, axis=0, keepdims=True))
-        p0, p1 = e0 * inv, e1 * inv
-        delta = jnp.sum(p0 * dp0, axis=0, keepdims=True) + jnp.sum(p1 * dp1, axis=0, keepdims=True)
-        p_s[own_rows, at] = p0.astype(BF)
-        p_s[other_rows, at] = p1.astype(BF)
-        d_s[own_rows, at] = (p0 * (dp0 - delta)).astype(BF)
-        d_s[other_rows, at] = (p1 * (dp1 - delta)).astype(BF)
-
-    def key_grad(half):
-        at = rows16(half * HALF, HALF)
-        a = jnp.dot(d_s[at, :], q_s[...], preferred_element_type=F32) * score_scale
-        b = jnp.dot(p_s[at, :], g_s[...], preferred_element_type=F32)
+        s, dp = s_s[:, at], dp_s[:, at]
+        e = jnp.exp2(s - jnp.max(s, axis=0, keepdims=True))
+        p = e * (1.0 / jnp.sum(e, axis=0, keepdims=True))
+        delta = jnp.sum(p * dp, axis=0, keepdims=True)
+        p_s[:, at] = p.astype(BF)
+        d_s[:, at] = (p * (dp - delta)).astype(BF)
+
+    def key_grad(rows):
+        a = jnp.dot(d_s[rows, :], q_s[...], preferred_element_type=F32) * score_scale
+        b = jnp.dot(p_s[rows, :], g_s[...], preferred_element_type=F32)
         return jnp.concatenate([a[:, 0:HL] + b, a[:, HL:]], axis=1)
 
-    kx_src[...] = key_grad(other).astype(BF)
+    kx_src[...] = key_grad(other_rows).astype(BF)
     kx = remote(kx_src, kx_buf, kx_send, kx_recv, sib)
     kx.start()
     drains.append(kx.wait_send)
-    kacc[...] = key_grad(core)
+    kacc[...] = key_grad(own_rows)
+    ko_acc[...] = key_grad(slice(2 * HALF, ROWS))
+    ko_src[...] = ko_acc[rows16(other * 64, 64), :].astype(BF)
+    ko = remote(ko_src, ko_buf, ko_send, ko_recv, sib)
+    ko.start()
+    drains.append(ko.wait_send)
     kx.wait_recv()
     total = kacc[...] + kx_buf[...].astype(F32)
     kacc[...] = total
-    xr_src[...] = total[0:256, :].astype(BF)
-    os_src[...] = total[256:HALF, :].astype(BF)
+    xr_src[...] = total.astype(BF)
 
     def xr(n):
         block = xr_src.at[rows16(plane(n, 1) * 16, 16)]
-        return remote(block, xr_buf.at[n], xr_send.at[n], xr_recv.at[n], at_xy(n))
+        return remote(block, xr_buf.at[n], xr_send, xr_recv, at_xy(n))
 
     for n in range(15):
         xr(n).start()
@@ -281,13 +276,9 @@
         block = ow_buf.at[rows16(core * 64 + src * 16, 16)]
         return remote(block, block, og_send.at[k], og_recv.at[src], (g, src * 2 + core))
 
-    for k in range(1, 4):
-        oz(k).start()
-    oz_buf[zl] = os_src[rows16(zl * 16, 16), :]
-
     def sums_sent():
-        for n in range(15):
-            xr(n).wait_send()
+        most = xr_src.at[0:240]
+        remote(most, most, xr_send, xr_recv, sib).wait_send()
         for k in range(1, 4):
             oz(k).wait_send()
 
@@ -300,8 +291,7 @@
             lw.at[hp],
         )
 
-    @pl.loop(0, HEADS // 2)
-    def _(hp):
+    def query_grad(hp):
         at = pl.ds(pl.multiple_of(hp * 256, 256), 256)
         tn = (((0,), (0,)), ((), ()))
         gq = lax.dot_general(d_s[:, at], k_s[...], tn, preferred_element_type=F32) * score_scale
@@ -311,7 +301,45 @@
         o_s[:, pl.ds(pl.multiple_of(hp * 2 * HK, 128), 2 * HK)] = joint.astype(BF)
         store_q(hp).start()
 
+    query_grad(0)
+    ko.wait_recv()
+    os_src[...] = (ko_acc[rows16(core * 64, 64), :] + ko_buf[...].astype(F32)).astype(BF)
+    for k in range(1, 4):
+        oz(k).start()
+    oz_buf[zl] = os_src[rows16(zl * 16, 16), :]
+    pl.loop(1, HEADS // 2)(query_grad)
+
     drains.append(lambda: [store_q(hp).wait() for hp in range(HEADS // 2)])
+    total = kacc[rows16(xy * 16, 16), :]
+    remote(xr_buf, xr_buf, xr_send, xr_recv, sib).wait_recv()
+    for n in range(15):
+        total = total + xr_buf[n].astype(F32)
+    zr_src[0] = pack(total[0:8, :]).astype(BF)
+    zr_src[1] = pack(total[8:16, :]).astype(BF)
+
+    pl.semaphore_wait(relay, 1)
+
+    def zr(i, a):
+        to = (core * 2 + i) * 4 + a
+        return remote(zr_src.at[i], zr_buf.at[z], zr_send, zr_recv, at_z(to))
+
+    for i in range(2):
+        for a in range(4):
+
+            @pl.when((core * 2 + i) * 4 + a != z)
+            def _():
+                zr(i, a).start()
+
+    def slabs_sent():
+        @pl.when(mine)
+        def _():
+            remote(zr_buf.at[0:7], zr_buf.at[0:7], zr_send, zr_recv, sib).wait_send()
+
+        @pl.when(jnp.logical_not(mine))
+        def _():
+            remote(zr_buf.at[0:8], zr_buf.at[0:8], zr_send, zr_recv, sib).wait_send()
+
+
     for k in range(1, 4):
         oz_from(k).wait_recv()
     own_sum = oz_buf[0].astype(F32)
@@ -321,39 +349,6 @@
     for k in range(1, 4):
         og(k).start()
     drains.append(lambda: [og(k).wait_send() for k in range(1, 4)])
-
-    total = kacc[rows16(xy * 16, 16), :]
-    for n in reversed(range(15)):
-        xr(n).wait_recv()
-        total = total + xr_buf[n].astype(F32)
-    zr_src[0] = pack(total[0:8, :]).astype(BF)
-    zr_src[1] = pack(total[8:16, :]).astype(BF)
-
-    pl.semaphore_wait(relay, 1)
-
-    def zr(i, a):
-        to = (core * 2 + i) * 4 + a
-        return remote(zr_src.at[i], zr_buf.at[z], zr_send.at[i * 4 + a], zr_recv.at[z], at_z(to))
-
-    def zr_from(src):
-        return remote(zr_src.at[0], zr_buf.at[src], zr_send.at[0], zr_recv.at[src], at_z(src))
-
-    for i in range(2):
-        for a in range(4):
-
-            @pl.when((core * 2 + i) * 4 + a != z)
-            def _():
-                zr(i, a).start()
-
-    def slabs_sent():
-        for i in range(2):
-            for a in range(4):
-
-                @pl.when((core * 2 + i) * 4 + a != z)
-                def _():
-                    zr(i, a).wait_send()
-
-    drains.append(slabs_sent)
 
     for k in range(1, 4):
         og_from(k).wait_recv()
@@ -368,24 +363,22 @@
     store_go.start()
     drains.append(store_go.wait)
 
+    for drain in drains:
+        drain()
+
     fin = remote(fin_src, fin_buf, fin_send, fin_recv, sib)
 
     @pl.when(mine)
     def _():
         zr_buf[z] = zr_src[zh % 2]
+        remote(zr_buf.at[0:15], zr_buf.at[0:15], zr_send, zr_recv, sib).wait_recv()
         total = jnp.zeros((16, 384), F32)
         for src in range(16):
-
-            @pl.when(z != src)
-            def _():
-                zr_from(src).wait_recv()
-
             total = total + zr_buf[src].astype(F32)
         whole = unpack(total)
         fin_src[...] = whole
         fin.start()
         gt_ref[...] = whole[:, 0:HK]
-        fin.wait_send()
 
     @pl.when(jnp.logical_not(mine))
     def _():
@@ -394,10 +387,13 @@
 
     store_gt = pltpu.make_async_copy(gt_ref, gt_hbm, lf.at[1])
     store_gt.start()
-    drains.append(store_gt.wait)
-
-    for drain in drains:
-        drain()
+    slabs_sent()
+
+    @pl.when(mine)
+    def _():
+        fin.wait_send()
+
+    store_gt.wait()
 
 
 def finish(q_in, t_in, o_in, q_out, t_out, o_out, q_s, t_s, o_s, sem, sem_out):
@@ -435,20 +431,23 @@
             pltpu.VMEM((HEADS * TOK, KP), BF),
             pltpu.VMEM((HEADS // 2 * TOK, KP), BF),
             pltpu.VMEM((HEADS * TOK, HL), BF),
-            pltpu.VMEM((2 * HALF, KP), BF),
-            pltpu.VMEM((2 * HALF, TOK), F32),
-            pltpu.VMEM((HALF, HEADS * TOK), F32),
-            pltpu.VMEM((HALF, HEADS * TOK), F32),
-            pltpu.VMEM((2 * HALF, HEADS * TOK), BF),
-            pltpu.VMEM((2 * HALF, HEADS * TOK), BF),
+            pltpu.VMEM((ROWS, KP), BF),
+            pltpu.VMEM((ROWS, TOK), F32),
+            pltpu.VMEM((ROWS, HEADS * TOK), F32),
+            pltpu.VMEM((ROWS, HEADS * TOK), F32),
+            pltpu.VMEM((ROWS, HEADS * TOK), BF),
+            pltpu.VMEM((ROWS, HEADS * TOK), BF),
             pltpu.VMEM((TOK, HEADS * HK), BF),
             pltpu.VMEM((16, 384), BF),
             pltpu.VMEM((4, 16, 384), BF),
             pltpu.VMEM((HALF, KP), BF),
             pltpu.VMEM((HALF, KP), BF),
             pltpu.VMEM((HALF, KP), F32),
-            pltpu.VMEM((256, KP), BF),
-            pltpu.VMEM((16, 16, KP), BF),
+            pltpu.VMEM((64, KP), BF),
+            pltpu.VMEM((64, KP), BF),
+            pltpu.VMEM((TOK, KP), F32),
+            pltpu.VMEM((HALF, KP), BF),
+            pltpu.VMEM((15, 16, KP), BF),
             pltpu.VMEM((2, 16, 384), BF),
             pltpu.VMEM((16, 16, 384), BF),
             pltpu.VMEM((8, KP), F32),
@@ -458,11 +457,11 @@
             pltpu.VMEM((TOK, KP), BF),
             dma((4,)), dma((4,)), dma((8,)), dma((4,)), dma((3,)), dma((2,)),
             dma((8,)), dma((4,)),
-            dma((16,)), dma((16,)),
-            dma((16,)), dma((16,)),
+            dma, dma((16,)),
             dma, dma,
-            dma((16,)), dma((16,)),
-            dma((8,)), dma((16,)),
+            dma, dma, dma, dma,
+            dma, dma,
+            dma, dma,
             dma, dma,
             dma((4,)), dma((4,)), dma((4,)), dma((4,)),
             dma, dma,

time: 55.5 us -> 53.7 us (0.968)
  Pallas kernels: 54.7 us -> 52.8 us
    pallas_call x1, Pallas kernels: 52.5 us -> 50.7 us  [per_device(): pl.pallas_call(kernel, out_shape=(jax.ShapeDtypeStruct((TOK, HEADS * HK),...]
where the time goes in v3:
time: 53.7 us; the launch traced here: 53.5 us
  Pallas kernels  52.8 us (98%)
  between operations  0.64 us (1%)
    pallas_call x1, Pallas kernels, per_device(): pl.pallas_call(kernel, out_shape=(jax.ShapeDtypeStruct((TOK, HEADS * HK),...  50.7 us
    pallas_call x1, Pallas kernels, per_device(): pl.pallas_call(finish, out_shape=outs, in_specs=[hbm] * 3, out_specs=[hbm...  2.17 us

profile of v3, /device:TPU:1, one launch (start us, length us, event | category | flops | bytes accessed | tf_op | source)
XLA Modules:
  0.0 53.5 jit_solution(17491132705956111421)
XLA Ops:
  0.6 50.7 %shard_map.76 = (bf16[128,4608]{1,0:T(8,128)(2,1)}, f32[8,576]{1,0:T(8,128)}, f32[576,128]{1,0:T(8,128)}) custom-call(bf16[128,4608]{1,0:T(8,128)(2,1)} %q_hbm.1, bf16[8,576]{1,0:T(8,128)(2,1)} %tr_hbm.1, bf16[576,128]{1,0:T(8,128)(2,1)} %bitcast.3, bf16[128,4096]{1,0:T(8,128)(2,1)} %g_hbm.1, s32[128]{0:T(128)} %vis_hbm.1), custom_call_target="tpu_custom_call" | custom-call | flops 3860000000 | bytes 4500000 | tf_op jit(solution)/shard_map/pallas_call | solution.py:416
  51.3 2.2 %shard_map.77 = (bf16[128,4608]{1,0:T(8,128)(2,1)}, f32[8,576]{1,0:T(8,128)}, f32[576,128]{1,0:T(8,128)}) custom-call(bf16[128,4608]{1,0:T(8,128)(2,1)} %get-tuple-element.9.q_in, f32[8,576]{1,0:T(8,128)} %get-tuple-element.10.t_in, f32[576,128]{1,0:T(8,128)} %get-tuple-element.11.o_in), custom_call_target="tpu_custom_call" | custom-call | tf_op jit(solution)/shard_map/pallas_call | solution.py:476

commit v4 on v3

--- a/solution.py
+++ b/solution.py
@@ -1,3 +1,5 @@
+import functools
+
 import jax
 import jax.numpy as jnp
 from jax import lax
@@ -169,13 +171,16 @@
 
     nt = (((1,), (1,)), ((), ()))
 
+    def score(rows, at):
+        s = lax.dot_general(k_s[rows, :], q_s[at, :], nt, preferred_element_type=F32)
+        dp = lax.dot_general(k_s[rows, 0:HL], g_s[at, :], nt, preferred_element_type=F32)
+        bias = jnp.concatenate([bias_s[rows, :], bias_s[rows, :]], axis=1)
+        return s * (score_scale * log2e) + bias, dp
+
     def scores(rows):
         for hp in range(HEADS // 2):
             at = slice(hp * 256, hp * 256 + 256)
-            s = lax.dot_general(k_s[rows, :], q_s[at, :], nt, preferred_element_type=F32)
-            bias = jnp.concatenate([bias_s[rows, :], bias_s[rows, :]], axis=1)
-            s_s[rows, at] = s * (score_scale * log2e) + bias
-            dp_s[rows, at] = lax.dot_general(k_s[rows, 0:HL], g_s[at, :], nt, preferred_element_type=F32)
+            s_s[rows, at], dp_s[rows, at] = score(rows, at)
 
     scores(slice(2 * HALF, ROWS))
 
@@ -189,25 +194,20 @@
     pair = jnp.concatenate([unpack(zg_buf[core * 2 + i].astype(F32)) for i in range(2)], axis=0)
     k_s[rows16(core * HALF + xy * 16, 16), :] = pair.astype(BF)
 
-    def xg(k):
+    def xg(n):
         block = k_s.at[rows16(core * HALF + xy * 16, 16)]
-        return remote(block, block, xg_send, xg_recv.at[k], at_xy(k))
-
-    def cg(n):
-        spot = xy if n == 15 else plane(n, -1)
-        block = k_s.at[rows16(core * HALF + spot * 16, 16)]
-        return remote(block, block, cg_send, cg_recv, sib)
-
-    def xg_got(n):
-        block = k_s.at[rows16(core * HALF + plane(n, -1) * 16, 16)]
-        return remote(block, block, xg_send, xg_recv.at[n], at_xy(n))
+        return remote(block, block, xg_send, xg_recv.at[PLANE[n][0]], at_xy(n))
+
+    def from_x(dx):
+        return k_s.at[rows16(core * HALF + ((xy // 4 + 4 - dx) % 4) * 64, 64)]
 
     for n in range(15):
         xg(n).start()
-    cg(15).start()
-    for n in reversed(range(15)):
-        xg_got(n).wait_recv()
-        cg(n).start()
+    for dx in (0, 1, 3, 2):
+        block = from_x(dx)
+        got = k_s.at[0:48] if dx == 0 else block
+        remote(got, got, xg_send, xg_recv.at[dx], sib).wait_recv()
+        remote(block, block, cg_send, cg_recv, sib).start()
     own_rows, other_rows = rows16(core * HALF, HALF), rows16(other * HALF, HALF)
 
     def keys_sent():
@@ -221,16 +221,18 @@
     scores(own_rows)
     half = k_s.at[other_rows]
     remote(half, half, cg_send, cg_recv, sib).wait_recv()
-    scores(other_rows)
-
+    rest = slice(2 * HALF, ROWS)
     for hp in range(HEADS // 2):
         at = slice(hp * 256, hp * 256 + 256)
-        s, dp = s_s[:, at], dp_s[:, at]
-        e = jnp.exp2(s - jnp.max(s, axis=0, keepdims=True))
-        p = e * (1.0 / jnp.sum(e, axis=0, keepdims=True))
-        delta = jnp.sum(p * dp, axis=0, keepdims=True)
-        p_s[:, at] = p.astype(BF)
-        d_s[:, at] = (p * (dp - delta)).astype(BF)
+        s, dp = zip((s_s[own_rows, at], dp_s[own_rows, at]), (s_s[rest, at], dp_s[rest, at]), score(other_rows, at))
+        top = functools.reduce(jnp.maximum, [jnp.max(a, axis=0, keepdims=True) for a in s])
+        e = [jnp.exp2(a - top) for a in s]
+        inv = 1.0 / sum(jnp.sum(a, axis=0, keepdims=True) for a in e)
+        p = [a * inv for a in e]
+        delta = sum(jnp.sum(a * b, axis=0, keepdims=True) for a, b in zip(p, dp))
+        for rows, a, b in zip((own_rows, rest, other_rows), p, dp):
+            p_s[rows, at] = a.astype(BF)
+            d_s[rows, at] = (a * (b - delta)).astype(BF)
 
     def key_grad(rows):
         a = jnp.dot(d_s[rows, :], q_s[...], preferred_element_type=F32) * score_scale
@@ -248,16 +250,17 @@
     ko.start()
     drains.append(ko.wait_send)
     kx.wait_recv()
-    total = kacc[...] + kx_buf[...].astype(F32)
-    kacc[...] = total
-    xr_src[...] = total.astype(BF)
 
     def xr(n):
         block = xr_src.at[rows16(plane(n, 1) * 16, 16)]
         return remote(block, xr_buf.at[n], xr_send, xr_recv, at_xy(n))
 
-    for n in range(15):
-        xr(n).start()
+    for dx in (2, 1, 3, 0):
+        group = rows16(((xy // 4 + dx) % 4) * 64, 64)
+        xr_src[group, :] = (kacc[group, :] + kx_buf[group, :].astype(F32)).astype(BF)
+        for n in range(15):
+            if PLANE[n][0] == dx:
+                xr(n).start()
 
     def oz(k):
         to = (zl + k) % 4
@@ -310,7 +313,8 @@
     pl.loop(1, HEADS // 2)(query_grad)
 
     drains.append(lambda: [store_q(hp).wait() for hp in range(HEADS // 2)])
-    total = kacc[rows16(xy * 16, 16), :]
+    spot = rows16(xy * 16, 16)
+    total = kacc[spot, :] + kx_buf[spot, :].astype(F32)
     remote(xr_buf, xr_buf, xr_send, xr_recv, sib).wait_recv()
     for n in range(15):
         total = total + xr_buf[n].astype(F32)
@@ -323,12 +327,21 @@
         to = (core * 2 + i) * 4 + a
         return remote(zr_src.at[i], zr_buf.at[z], zr_send, zr_recv, at_z(to))
 
-    for i in range(2):
+    near = zh % 2
+
+    @pl.when(mine)
+    def _():
         for a in range(4):
-
-            @pl.when((core * 2 + i) * 4 + a != z)
-            def _():
-                zr(i, a).start()
+            zr(1 - near, a).start()
+        for k in range(1, 4):
+            zr(near, (zl + k) % 4).start()
+
+    @pl.when(jnp.logical_not(mine))
+    def _():
+        for a in range(4):
+            zr(near, a).start()
+        for a in range(4):
+            zr(1 - near, a).start()
 
     def slabs_sent():
         @pl.when(mine)
@@ -457,7 +470,7 @@
             pltpu.VMEM((TOK, KP), BF),
             dma((4,)), dma((4,)), dma((8,)), dma((4,)), dma((3,)), dma((2,)),
             dma((8,)), dma((4,)),
-            dma, dma((16,)),
+            dma, dma((4,)),
             dma, dma,
             dma, dma, dma, dma,
             dma, dma,

time: 53.7 us -> 54.1 us (level)
  no operation moved by 1% of the time
where the time goes in v4:
time: 54.1 us; the launch traced here: 53.9 us
  Pallas kernels  53.2 us (98%)
  between operations  0.64 us (1%)
    pallas_call x1, Pallas kernels, per_device(): pl.pallas_call(kernel, out_shape=(jax.ShapeDtypeStruct((TOK, HEADS * HK),...  51.1 us
    pallas_call x1, Pallas kernels, per_device(): pl.pallas_call(finish, out_shape=outs, in_specs=[hbm] * 3, out_specs=[hbm...  2.17 us

profile of v4, /device:TPU:1, one launch (start us, length us, event | category | flops | bytes accessed | tf_op | source)
XLA Modules:
  0.0 53.9 jit_solution(9733424433978570138)
XLA Ops:
  0.6 51.1 %shard_map.76 = (bf16[128,4608]{1,0:T(8,128)(2,1)}, f32[8,576]{1,0:T(8,128)}, f32[576,128]{1,0:T(8,128)}) custom-call(bf16[128,4608]{1,0:T(8,128)(2,1)} %q_hbm.1, bf16[8,576]{1,0:T(8,128)(2,1)} %tr_hbm.1, bf16[576,128]{1,0:T(8,128)(2,1)} %bitcast.3, bf16[128,4096]{1,0:T(8,128)(2,1)} %g_hbm.1, s32[128]{0:T(128)} %vis_hbm.1), custom_call_target="tpu_custom_call" | custom-call | flops 3860000000 | bytes 4500000 | tf_op jit(solution)/shard_map/pallas_call | solution.py:429
  51.7 2.2 %shard_map.77 = (bf16[128,4608]{1,0:T(8,128)(2,1)}, f32[8,576]{1,0:T(8,128)}, f32[576,128]{1,0:T(8,128)}) custom-call(bf16[128,4608]{1,0:T(8,128)(2,1)} %get-tuple-element.9.q_in, f32[8,576]{1,0:T(8,128)} %get-tuple-element.10.t_in, f32[576,128]{1,0:T(8,128)} %get-tuple-element.11.o_in), custom_call_target="tpu_custom_call" | custom-call | tf_op jit(solution)/shard_map/pallas_call | solution.py:489

commit v5 on v3

--- a/solution.py
+++ b/solution.py
@@ -355,14 +355,6 @@
     own_half = ow_buf.at[rows16(core * 64, 64)]
     fo = remote(own_half, own_half, fo_send, fo_recv, sib)
     fo.start()
-    drains.append(fo.wait_send)
-    own_half = ow_buf.at[rows16(other * 64, 64)]
-    remote(own_half, own_half, fo_send, fo_recv, sib).wait_recv()
-    got_ref[...] = ow_buf[...].astype(F32).T[0:HK, :]
-    store_go = pltpu.make_async_copy(got_ref, go_hbm, lf.at[0])
-    store_go.start()
-    drains.append(store_go.wait)
-
     for drain in drains:
         drain()
 
@@ -380,6 +372,12 @@
         fin.start()
         gt_ref[...] = whole[:, 0:HK]
 
+    own_half = ow_buf.at[rows16(other * 64, 64)]
+    remote(own_half, own_half, fo_send, fo_recv, sib).wait_recv()
+    got_ref[...] = ow_buf[...].astype(F32).T[0:HK, :]
+    store_go = pltpu.make_async_copy(got_ref, go_hbm, lf.at[0])
+    store_go.start()
+
     @pl.when(jnp.logical_not(mine))
     def _():
         fin.wait_recv()
@@ -393,6 +391,8 @@
     def _():
         fin.wait_send()
 
+    fo.wait_send()
+    store_go.wait()
     store_gt.wait()
 
 

time: 53.7 us -> 53.7 us (level)
  no operation moved by 1% of the time
where the time goes in v5:
time: 53.7 us; the launch traced here: 53.5 us
  Pallas kernels  52.8 us (98%)
  between operations  0.64 us (1%)
    pallas_call x1, Pallas kernels, per_device(): pl.pallas_call(kernel, out_shape=(jax.ShapeDtypeStruct((TOK, HEADS * HK),...  50.7 us
    pallas_call x1, Pallas kernels, per_device(): pl.pallas_call(finish, out_shape=outs, in_specs=[hbm] * 3, out_specs=[hbm...  2.17 us

profile of v5, /device:TPU:1, one launch (start us, length us, event | category | flops | bytes accessed | tf_op | source)
XLA Modules:
  0.0 53.5 jit_solution(7922895672714939975)
XLA Ops:
  0.6 50.7 %shard_map.76 = (bf16[128,4608]{1,0:T(8,128)(2,1)}, f32[8,576]{1,0:T(8,128)}, f32[576,128]{1,0:T(8,128)}) custom-call(bf16[128,4608]{1,0:T(8,128)(2,1)} %q_hbm.1, bf16[8,576]{1,0:T(8,128)(2,1)} %tr_hbm.1, bf16[576,128]{1,0:T(8,128)(2,1)} %bitcast.3, bf16[128,4096]{1,0:T(8,128)(2,1)} %g_hbm.1, s32[128]{0:T(128)} %vis_hbm.1), custom_call_target="tpu_custom_call" | custom-call | flops 3860000000 | bytes 4500000 | tf_op jit(solution)/shard_map/pallas_call | solution.py:416
  51.3 2.2 %shard_map.77 = (bf16[128,4608]{1,0:T(8,128)(2,1)}, f32[8,576]{1,0:T(8,128)}, f32[576,128]{1,0:T(8,128)}) custom-call(bf16[128,4608]{1,0:T(8,128)(2,1)} %get-tuple-element.9.q_in, f32[8,576]{1,0:T(8,128)} %get-tuple-element.10.t_in, f32[576,128]{1,0:T(8,128)} %get-tuple-element.11.o_in), custom_call_target="tpu_custom_call" | custom-call | tf_op jit(solution)/shard_map/pallas_call | solution.py:476

commit v6 on v5

--- a/solution.py
+++ b/solution.py
@@ -105,45 +105,45 @@
     small[0].wait()
     slab = jnp.concatenate([tr_ref[...].astype(F32), jnp.zeros((8, KP - HK), F32)], axis=1)
     zg_src[...] = pack(slab).astype(BF)
-    mine = (zh // 2) == core
-
-    pl.semaphore_wait(barrier, 28)
-
-    def zg(d, up):
-        zz = (z + d) % 16 if up else (z + 16 - d) % 16
-        return remote(zg_src, zg_buf.at[zh], zg_send.at[d], zg_recv.at[zh], at_z(zz))
-
-    def zg_from(src):
-        return remote(zg_src, zg_buf.at[src], zg_send.at[0], zg_recv.at[src], (g, t))
-
-    for chip, up in ((3, True), (0, False)):
-
-        @pl.when(jnp.logical_and(mine, zl == chip))
-        def _():
-            for d in reversed(range(1, 7)):
-                zg(d, up).start()
-
-    @pl.when(mine)
-    def _():
-        zg_buf[zh] = zg_src[...]
-
-    def zg_sent():
-        for chip, up in ((3, True), (0, False)):
-
-            @pl.when(jnp.logical_and(mine, zl == chip))
-            def _():
-                for d in range(1, 7):
-                    zg(d, up).wait_send()
-
-    drains = [zg_sent]
-
-    pl.semaphore_signal(relay, inc=1, device_id=at_z((z + 10) % 16), device_id_type=MESH)
-
     for hp in range(HEADS // 2):
         load_q(hp).start()
         load_o(hp).start()
     for h in range(HEADS):
         load_g(h).start()
+    mine = (zh // 2) == core
+
+    pl.semaphore_wait(barrier, 28)
+
+    def zg(d, up):
+        zz = (z + d) % 16 if up else (z + 16 - d) % 16
+        return remote(zg_src, zg_buf.at[zh], zg_send.at[d], zg_recv.at[zh], at_z(zz))
+
+    def zg_from(src):
+        return remote(zg_src, zg_buf.at[src], zg_send.at[0], zg_recv.at[src], (g, t))
+
+    for chip, up in ((3, True), (0, False)):
+
+        @pl.when(jnp.logical_and(mine, zl == chip))
+        def _():
+            for d in reversed(range(1, 7)):
+                zg(d, up).start()
+
+    @pl.when(mine)
+    def _():
+        zg_buf[zh] = zg_src[...]
+
+    def zg_sent():
+        for chip, up in ((3, True), (0, False)):
+
+            @pl.when(jnp.logical_and(mine, zl == chip))
+            def _():
+                for d in range(1, 7):
+                    zg(d, up).wait_send()
+
+    drains = [zg_sent]
+
+    pl.semaphore_signal(relay, inc=1, device_id=at_z((z + 10) % 16), device_id_type=MESH)
+
     small[1].wait()
     owns = own_ref[...].astype(F32).T.astype(BF)
     k_s[2 * HALF : ROWS, :] = jnp.concatenate([owns, jnp.zeros((TOK, KP - HK), BF)], axis=1)

time: 53.7 us -> 53.6 us (level)
  no operation moved by 1% of the time
where the time goes in v6:
time: 53.6 us; the launch traced here: 53.5 us
  Pallas kernels  52.8 us (99%)
  between operations  0.64 us (1%)
    pallas_call x1, Pallas kernels, per_device(): pl.pallas_call(kernel, out_shape=(jax.ShapeDtypeStruct((TOK, HEADS * HK),...  50.7 us
    pallas_call x1, Pallas kernels, per_device(): pl.pallas_call(finish, out_shape=outs, in_specs=[hbm] * 3, out_specs=[hbm...  2.17 us

profile of v6, /device:TPU:1, one launch (start us, length us, event | category | flops | bytes accessed | tf_op | source)
XLA Modules:
  0.0 53.5 jit_solution(13098739038087594310)
XLA Ops:
  0.6 50.7 %shard_map.76 = (bf16[128,4608]{1,0:T(8,128)(2,1)}, f32[8,576]{1,0:T(8,128)}, f32[576,128]{1,0:T(8,128)}) custom-call(bf16[128,4608]{1,0:T(8,128)(2,1)} %q_hbm.1, bf16[8,576]{1,0:T(8,128)(2,1)} %tr_hbm.1, bf16[576,128]{1,0:T(8,128)(2,1)} %bitcast.3, bf16[128,4096]{1,0:T(8,128)(2,1)} %g_hbm.1, s32[128]{0:T(128)} %vis_hbm.1), custom_call_target="tpu_custom_call" | custom-call | flops 3860000000 | bytes 4500000 | tf_op jit(solution)/shard_map/pallas_call | solution.py:416
  51.3 2.2 %shard_map.77 = (bf16[128,4608]{1,0:T(8,128)(2,1)}, f32[8,576]{1,0:T(8,128)}, f32[576,128]{1,0:T(8,128)}) custom-call(bf16[128,4608]{1,0:T(8,128)(2,1)} %get-tuple-element.9.q_in, f32[8,576]{1,0:T(8,128)} %get-tuple-element.10.t_in, f32[576,128]{1,0:T(8,128)} %get-tuple-element.11.o_in), custom_call_target="tpu_custom_call" | custom-call | tf_op jit(solution)/shard_map/pallas_call | solution.py:476
